TPU v7x, 256 devices: a whole 4x4x8 slice. The times are simulated.
256 devices in a mesh: ctx: 16 (over z, core), head: 16 (over y, x).
Axes of the slice: x: 4, y: 4, z: 8, core: 2. Of those that a mesh axis runs over, the one named last changes fastest.
Arguments:
- queries: bfloat16 [16384, 8192], P('ctx', 'head'), may hold values from -0.59765625 to 0.59765625
- keys: bfloat16 [16384, 8192], P('ctx', 'head'), may hold values from -0.59765625 to 0.59765625
- values: bfloat16 [16384, 8192], P('ctx', 'head'), may hold values from -0.59765625 to 0.59765625
- out_grad: bfloat16 [16384, 8192], P(('ctx', 'head')), may hold values from -0.59765625 to 0.59765625
- state_in: float32 [64, 128, 128], P('head'), may hold values from -6 to 6
- exponents: int32 [64], P('head'), may hold values from 1 to 4095, as said below
- boundaries: int32 [8], replicated, may hold values from 1 to 16383
Outputs:
- query_grad: bfloat16 [16384, 8192], P('ctx', 'head')
- key_grad: bfloat16 [16384, 8192], P('ctx', 'head')
- value_grad: bfloat16 [16384, 8192], P('ctx', 'head')
- state_grad: float32 [64, 128, 128], P('head', 'ctx')
Inputs may be any that keep to these rules, and one draw needn't show every extreme that they name: `exponents`: each head's exponent is a whole number; larger ones forget faster. `boundaries`: positions may repeat; each occurrence halves the state once more.
All inputs are finite; a program needn't handle non-finite values.
Results may differ from a plain program's by a relative error of at most 0.009.
Values may be sent and summed in bfloat16 or wider, within the bound.
A program may use at most 64 MiB of HBM per device.

v0:
```python
import jax
import jax.numpy as jnp
from jax import lax
from jax.sharding import PartitionSpec as P

D_HEAD = 128
BLOCK = 256


def entering(x, axis, combine, identity):
    count, mine = (lax.axis_size(axis), lax.axis_index(axis))
    everything = jax.tree.map(
        lambda part, kind: lax.all_gather(part.astype(kind), axis), x, (jnp.bfloat16, jnp.bfloat16)
    )
    start = jax.tree.map(
        lambda part, zero: jnp.broadcast_to(jnp.asarray(zero, part.dtype), part.shape), x, identity
    )

    def turn(k, before):
        reached = k < mine
        new = combine(
            before, jax.tree.map(lambda part, own: part[k].astype(own.dtype), everything, x)
        )
        return jax.tree.map(lambda a, b: jnp.where(reached, a, b), new, before)

    return lax.fori_loop(0, count, turn, start)


def entering_2(part, axis, combine, identity):
    count = lax.axis_size(axis)
    place = lax.axis_index(axis)
    ahead = count - 1 - place
    gathered = jax.tree.map(lambda a: lax.all_gather(a, axis), part)
    state = jax.tree.map(lambda a, e: jnp.zeros_like(a) + jnp.asarray(e, a.dtype), part, identity)

    def one(turn, state):
        source = count - 1 - turn
        return combine(
            state, jax.tree.map(lambda a: lax.dynamic_index_in_dim(a, source, 0, False), gathered)
        )

    return lax.fori_loop(0, ahead, one, state)


def from_root(value, axis, source):
    kept = jnp.where(lax.axis_index(axis) == source, value, 0).astype(value.dtype)
    return lax.psum(kept, axis)


def mix(form, left, right):
    return jnp.einsum(form, left, right, precision=lax.Precision.HIGHEST)


def block_rates(exponents, boundaries, start, block, total):
    offsets = jnp.arange(block, dtype=jnp.int32)
    places = start + offsets
    hits = jnp.sum((boundaries[:, None] == places[None, :]).astype(jnp.float32), axis=0)
    linear = (exponents[:, None] * (offsets[None, :] + 1)).astype(jnp.float32) / (4.0 * total)
    return -linear - jnp.cumsum(hits)[None, :]


def block_states(qb, kb, vb, gb, rates):
    head_in = jnp.exp2(rates)[..., None]
    tail_out = jnp.exp2(rates[:, -1:] - rates)[..., None]
    own_state = mix("hjd,hje->hde", kb.astype(jnp.float32) * tail_out, vb.astype(jnp.float32))
    own_grad = mix("hid,hie->hde", qb.astype(jnp.float32) * head_in, gb.astype(jnp.float32))
    return (own_state, own_grad, rates[:, -1])


def block_terms(qb, kb, vb, gb, rates, prev_state, following_grad):
    size = rates.shape[1]
    spread = rates[:, :, None] - rates[:, None, :]
    lower = jnp.arange(size)[:, None] >= jnp.arange(size)[None, :]
    weight = jnp.where(lower[None], jnp.exp2(jnp.minimum(spread, 0.0)), 0.0)
    pair_grad = jnp.einsum("hie,hje->hij", gb, vb, preferred_element_type=jnp.float32) * weight
    pair_key = jnp.einsum("hid,hjd->hij", qb, kb, preferred_element_type=jnp.float32) * weight
    qf = qb.astype(jnp.float32)
    kf = kb.astype(jnp.float32)
    vf = vb.astype(jnp.float32)
    gf = gb.astype(jnp.float32)
    head_in = jnp.exp2(rates)[..., None]
    tail_out = jnp.exp2(rates[:, -1:] - rates)[..., None]
    dquery = mix("hij,hjd->hid", pair_grad, kf) + head_in * mix("hie,hde->hid", gf, prev_state)
    dkey = mix("hij,hid->hjd", pair_grad, qf) + tail_out * mix("hje,hde->hjd", vf, following_grad)
    dvalue = mix("hij,hie->hje", pair_key, gf) + tail_out * mix("hjd,hde->hje", kf, following_grad)
    return (dquery, dkey, dvalue)


def merge_decayed_states(earlier, later):
    return (earlier[0] + later[0], jnp.exp2(later[0])[:, None, None] * earlier[1] + later[1])


def shards(queries, keys, values, out_grad, state_in, exponents, boundaries):
    tokens_here = queries.shape[0]
    heads_here = queries.shape[1] // D_HEAD
    count = tokens_here // BLOCK
    cotangent = lax.all_to_all(out_grad, "head", split_axis=1, concat_axis=0, tiled=True)
    total = lax.axis_size("ctx") * tokens_here
    position = lax.axis_index("ctx")
    start = position * tokens_here
    blocked = tuple(
        (
            whole.reshape(count, BLOCK, heads_here, D_HEAD).transpose(0, 2, 1, 3)
            for whole in (queries, keys, values, cotangent)
        )
    )

    def pieces(index):
        return [lax.dynamic_index_in_dim(whole, index, 0, keepdims=False) for whole in blocked]

    def own_terms(carry, index):
        qb, kb, vb, gb = pieces(index)
        rates = block_rates(exponents, boundaries, start + index * BLOCK, BLOCK, total)
        return (carry, block_states(qb, kb, vb, gb, rates))

    indices = jnp.arange(count, dtype=jnp.int32)
    _, (own_states, segment_own_grads, lasts) = lax.scan(own_terms, None, indices)
    empty = jnp.zeros((heads_here, D_HEAD, D_HEAD), jnp.float32)

    def forward(state, item):
        own_state, last = item
        return (jnp.exp2(last)[:, None, None] * state + own_state, state)

    local_state, local_prev = lax.scan(forward, empty, (own_states, lasts))

    def backward(grad, item):
        own_grad, last = item
        return (own_grad + jnp.exp2(last)[:, None, None] * grad, grad)

    segment_grad, local_next = lax.scan(backward, empty, (segment_own_grads, lasts), reverse=True)
    inclusive = jnp.cumsum(lasts, axis=0)
    decay_here = inclusive[-1]
    before = inclusive - lasts
    after = decay_here[None, :] - inclusive
    rows = D_HEAD // lax.axis_size("ctx")
    identity = (jnp.zeros((heads_here,), jnp.float32), empty)
    fore = entering((decay_here, local_state), "ctx", merge_decayed_states, identity)
    preceding_decay = fore[0]
    incoming = fore[1] + jnp.exp2(preceding_decay)[:, None, None] * state_in
    back = entering_2((decay_here, segment_grad), "ctx", merge_decayed_states, identity)
    incoming_grad = back[1]
    whole_grad = segment_grad + jnp.exp2(decay_here)[:, None, None] * incoming_grad
    start_total = from_root(whole_grad, "ctx", 0)
    state_grad = lax.dynamic_slice_in_dim(start_total, position * rows, rows, 1)
    prev_states = local_prev + jnp.exp2(before)[:, :, None, None] * incoming[None]
    next_grads = local_next + jnp.exp2(after)[:, :, None, None] * incoming_grad[None]

    def finish(carry, item):
        index, prev_state, following_grad = item
        qb, kb, vb, gb = pieces(index)
        rates = block_rates(exponents, boundaries, start + index * BLOCK, BLOCK, total)
        outs = block_terms(qb, kb, vb, gb, rates, prev_state, following_grad)
        return (carry, tuple((o.astype(jnp.bfloat16) for o in outs)))

    _, (dquery, dkey, dvalue) = lax.scan(finish, None, (indices, prev_states, next_grads))
    shape = (tokens_here, heads_here * D_HEAD)
    dquery = dquery.transpose(0, 2, 1, 3).reshape(shape)
    dkey = dkey.transpose(0, 2, 1, 3).reshape(shape)
    dvalue = dvalue.transpose(0, 2, 1, 3).reshape(shape)
    return (dquery, dkey, dvalue, state_grad)


def solution(mesh):
    in_specs = (
        P("ctx", "head"),
        P("ctx", "head"),
        P("ctx", "head"),
        P(("ctx", "head"), None),
        P("head", None, None),
        P("head"),
        P(),
    )
    out_specs = (P("ctx", "head"), P("ctx", "head"), P("ctx", "head"), P("head", "ctx", None))
    return jax.shard_map(shards, mesh=mesh, in_specs=in_specs, out_specs=out_specs, check_vma=False)
```

profile of v0, /device:TPU:1, one launch (start us, length us, event | category | flops | bytes accessed | tf_op | source)
XLA Modules:
  0.0 352.3 jit_solution(9876074136472468615)
XLA Ops:
  7.2 2.4 copy.159
  9.6 7.6 %all-to-all-start = ((bf16[64,16,512]{2,0,1:T(8,128)(2,1)}), bf16[64,16,512]{2,0,1:T(8,128)(2,1)S(1)}, u32[]{:S(2)}, u32[]{:S(2)}) async-start(bf16[64,16,512]{2,0,1:T(8,128)(2,1)} %bitcast.138), calls=%async_computation | async-start | bytes 2097152 | tf_op jit(solution)/shard_map/all_to_all | solution.py:97
  17.8 2.2 reshape.473
  19.9 2.2 reshape.474
  22.1 11.0 %all-to-all-done = bf16[64,16,512]{2,0,1:T(8,128)(2,1)S(1)} async-done(((bf16[64,16,512]{2,0,1:T(8,128)(2,1)}), bf16[64,16,512]{2,0,1:T(8,128)(2,1)S(1)}, u32[]{:S(2)}, u32[]{:S(2)}) %all-to-all-start) | async-done | bytes 1048608 | tf_op jit(solution)/shard_map/all_to_all | solution.py:97
  34.7 1.1 broadcast.352.clone.2
  35.8 32.3 %while.88 = (s32[]{:T(128)}, f32[4,4,128,128]{3,2,1,0:T(8,128)}, f32[4,4,128,128]{3,2,1,0:T(8,128)}, f32[4,4]{1,0:T(4,128)S(1)}, s32[4]{0:T(128)S(1)}, /*index=5...) while((s32[]{:T(128)}, f32[4,4,128,128]{3,2,1,0:T(8,128)}, ...), condition=%wide.region_4.5_spmd, body=%wide.region_0.4_spmd.sunk | while | flops 403229952 | bytes 3704267 | solution.py:117
  40.1 1.2 constant_dynamic-slice_fusion.10
  41.5 1.1 fusion.78
  42.8 1.1 fusion.77
  48.2 1.2 constant_dynamic-slice_fusion.10
  49.6 1.1 fusion.78
  50.8 1.1 fusion.77
  56.2 1.2 constant_dynamic-slice_fusion.10
  57.6 1.1 fusion.78
  58.9 1.1 fusion.77
  64.3 1.2 constant_dynamic-slice_fusion.10
  65.7 1.1 fusion.78
  67.0 1.1 fusion.77
  68.3 4.5 %while.91 = (s32[]{:T(128)}, f32[4,128,128]{2,1,0:T(8,128)S(1)}, f32[4,4,128,128]{3,2,1,0:T(8,128)S(1)}, f32[4,4]{1,0:T(4,128)S(1)}, f32[4,4,128,128]{3,2,1,0:T(8,128)}, /*index=5*/s32[]{:T(128)}, s32[]{:T(128)}) while((s32[]{:T(128)}, f32[4,128,128]{2,1,0:T(8,128)S(1)}, f32[4,4,128,128]{3,2,1,0:T(8,128)S(1)}, ...), condition=%wide.region_6.7_spmd.clone, body=%wide.region_5.6_spmd.clone.sunk | while | flops 262151 | bytes 1310868 | solution.py:124
  73.9 22.3 %all-gather.2 = bf16[16,1,4]{2,1,0:T(2,128)(2,1)S(1)} all-gather(bf16[1,1,4]{2,1,0:T(2,128)(2,1)S(1)} %convert_bitcast_fusion), channel_id=1, replica_groups=mesh['ctx'=16,'head'=16] {'ctx'}, dimensions={0}, use_global_device_ids=true | all-gather | bytes 136 | tf_op jit(solution)/shard_map/all_gather | solution.py:13
  96.4 14.3 %all-gather.3 = f32[16,1,4]{2,1,0:T(1,128)S(1)} all-gather(f32[1,1,4]{2,1,0:T(1,128)S(1)} %get-tuple-element.853), channel_id=1, replica_groups=mesh['ctx'=16,'head'=16] {'ctx'}, dimensions={0}, use_global_device_ids=true | all-gather | bytes 272 | tf_op jit(solution)/shard_map/all_gather | solution.py:33
  111.8 7.2 %while.93 = (s32[]{:T(128)}, f32[4,128,128]{2,1,0:T(8,128)S(1)}, f32[4,4,128,128]{3,2,1,0:T(8,128)}, f32[4,4,128,128]{3,2,1,0:T(8,128)}, f32[4,4]{1,0:T(4,128)S(1)}, /*index=5*/s32[]{:T(128)}, s32[]{:T(128)}, s32[]{:T(128)}) while((s32[]{:T(128)}, f32[4,128,128]{2,1,0:T(8,128)S(1)}, f32[4,4,128,128]{3,2,1,0:T(8,128)}, ...), condition=%wide.region_11.12_spmd.clone, body=%wide.region_10.11_spmd.clone.sunk | while | flops 262152 | bytes 1310888 | solution.py:130
  119.8 17.1 %while.92 = (s32[]{:T(128)}, f32[4]{0:T(128)S(1)}, f32[4,128,128]{2,1,0:T(8,128)S(1)}, s32[]{:T(128)}, bf16[16,4]{1,0:T(8,128)(2,1)S(1)}, /*index=5*/bf16[16,4,128,128]{3,2,1,0:T(8,128)(2,1)}, s32[]{:T(128)}, s32[]{:T(128)}) while((s32[]{:T(128)}, f32[4]{0:T(128)S(1)}, f32[4,128,128]{2,1,0:T(8,128)S(1)}, s32[]{:T(128)}, ...), condition=%wide.region_9.10_spmd.clone, body=%wide.region_8.9_spmd.clone.sunk | while | flops 327704 | bytes 655547 | solution.py:26
  138.0 1.1 multiply_add_fusion.1
  139.1 17.6 %all-gather.9.cloned.1.call-done = f32[64,128,128]{2,1,0:T(8,128)} async-done(((f32[4,128,128]{2,1,0:T(8,128)}), f32[64,128,128]{2,1,0:T(8,128)}) %all-gather.9.cloned.1.call-update) | async-done | bytes 4194320 | tf_op jit(solution)/shard_map/all_gather | solution.py:33
  156.8 15.7 %while.89 = (s32[]{:T(128)}, f32[4,128,128]{2,1,0:T(8,128)S(1)}, s32[]{:T(128)}, f32[16,4]{1,0:T(8,128)S(1)}, f32[16,4,128,128]{3,2,1,0:T(8,128)}, /*index=5*/s32[]{:T(128)}, s32[]{:T(128)}, s32[]{:T(128)}, s32[]{:T(128)}) while((s32[]{:T(128)}, f32[4,128,128]{2,1,0:T(8,128)S(1)}, s32[]{:T(128)}, f32[16,4]{1,0:T(8,128)S(1)}, ...), condition=%wide.region_13.14_spmd, body=%wide.region_12.13_spmd.sunk | while | flops 131082 | bytes 786627 | solution.py:42
  172.5 1.2 multiply_add_fusion
  173.7 60.4 %while.90 = (s32[]{:T(128)}, bf16[4,4,256,128]{3,2,1,0:T(8,128)(2,1)}, bf16[4,4,256,128]{3,2,1,0:T(8,128)(2,1)}, bf16[4,4,256,128]{3,2,1,0:T(8,128)(2,1)}, s32[4...) while((s32[]{:T(128)}, ...), condition=%wide.region_18.19_spmd, body=%wide.region_14.18_spmd.sunk | while | flops 1950076160 | bytes 13881787 | solution.py:155
  176.2 1.2 constant_dynamic-slice_fusion.11
  179.5 1.3 convolution_multiply_fusion.13
  180.9 1.8 fusion.92
  183.0 1.3 convolution_multiply_fusion.12
  184.3 1.8 fusion.91
  186.1 1.3 convolution_multiply_fusion.10
  187.4 1.3 fusion.90
  191.3 1.2 constant_dynamic-slice_fusion.11
  194.7 1.3 convolution_multiply_fusion.13
  196.0 1.8 fusion.92
  198.1 1.3 convolution_multiply_fusion.12
  199.5 1.8 fusion.91
  201.2 1.3 convolution_multiply_fusion.10
  202.6 1.3 fusion.90
  206.4 1.2 constant_dynamic-slice_fusion.11
  209.8 1.3 convolution_multiply_fusion.13
  211.1 1.8 fusion.92
  213.2 1.3 convolution_multiply_fusion.12
  214.6 1.8 fusion.91
  216.3 1.3 convolution_multiply_fusion.10
  217.7 1.3 fusion.90
  221.5 1.2 constant_dynamic-slice_fusion.11
  224.9 1.3 convolution_multiply_fusion.13
  226.2 1.8 fusion.92
  228.3 1.3 convolution_multiply_fusion.12
  229.7 1.8 fusion.91
  231.4 1.3 convolution_multiply_fusion.10
  232.8 1.3 fusion.90
  234.1 2.1 copy.134
  236.2 2.0 copy.135
  239.1 1.7 copy_bitcast_fusion.7
  240.7 2.0 copy.133
  242.8 1.2 copy.158
  243.9 100.5 %all-reduce.2.cloned.1.call-done = f32[4,128,128]{2,1,0:T(8,128)} async-done(((f32[4,128,128]{2,1,0:T(8,128)}), f32[4,128,128]{2,1,0:T(8,128)}) %all-reduce.2.cloned.1.call-update) | async-done | bytes 262160 | tf_op jit(solution)/shard_map/psum | solution.py:47
  344.4 1.3 constant_dynamic-slice_fusion.7
  (256 shorter events, 68.4 us)
Async XLA Ops:
  7.2 10.1 %copy-start.5 = (bf16[1024,512]{1,0:T(8,128)(2,1)S(1)}, bf16[1024,512]{1,0:T(8,128)(2,1)}, u32[]{:S(2)}) copy-start(bf16[1024,512]{1,0:T(8,128)(2,1)} %param.21) | copy-start | bytes 3145732
  9.6 23.6 %all-to-all-start = ((bf16[64,16,512]{2,0,1:T(8,128)(2,1)}), bf16[64,16,512]{2,0,1:T(8,128)(2,1)S(1)}, u32[]{:S(2)}, u32[]{:S(2)}) async-start(bf16[64,16,512]{2,0,1:T(8,128)(2,1)} %bitcast.138), calls=%async_computation | async-start | bytes 2097152 | tf_op jit(solution)/shard_map/all_to_all | solution.py:97
  17.2 102.7 %all-gather.7.cloned.1.call-start = ((), (), s32[]{:S(2)}) async-start(), calls=%async_computation.2 | async-start | bytes 2228224 | tf_op jit(solution)/shard_map/all_gather | solution.py:13
  19.9 15.9 %copy-start.6 = (s32[4]{0:T(128)S(1)}, s32[4]{0:T(128)}, u32[]{:S(2)}) copy-start(s32[4]{0:T(128)} %param.24) | copy-start | bytes 52
  19.9 15.9 %copy-start.7 = (s32[8]{0:T(128)S(1)}, s32[8]{0:T(128)}, u32[]{:S(2)}) copy-start(s32[8]{0:T(128)} %param.25) | copy-start | bytes 100
  72.7 1.1 copy-start.2
  73.5 83.2 %all-gather.9.cloned.1.call-start = ((), (), s32[]{:S(2)}) async-start(), calls=%async_computation.3 | async-start | bytes 4456448 | tf_op jit(solution)/shard_map/all_gather | solution.py:33
  119.0 0.7 copy-start
  119.7 18.2 %copy-start.3 = (f32[4,4,128,128]{3,2,1,0:T(8,128)S(1)}, f32[4,4,128,128]{3,2,1,0:T(8,128)}, u32[]{:S(2)}) copy-start(f32[4,4,128,128]{3,2,1,0:T(8,128)} %copy-done.2) | copy-start | bytes 3145732
  119.8 224.7 %all-reduce.2.cloned.1.call-start = ((), (), s32[]{:S(2)}) async-start(), calls=%async_computation.1 | async-start | bytes 524288 | tf_op jit(solution)/shard_map/psum | solution.py:47
  139.1 33.4 %copy-start.4 = (f32[4,4,128,128]{3,2,1,0:T(8,128)S(1)}, f32[4,4,128,128]{3,2,1,0:T(8,128)}, u32[]{:S(2)}) copy-start(f32[4,4,128,128]{3,2,1,0:T(8,128)} %get-tuple-element.475) | copy-start | bytes 3145732
  234.1 4.1 %copy-start.1 = (f32[4,128,128]{2,1,0:T(8,128)S(1)}, f32[4,128,128]{2,1,0:T(8,128)}, u32[]{:S(2)}) copy-start(f32[4,128,128]{2,1,0:T(8,128)} %copy-done) | copy-start | bytes 786436
Sparse Core Ops, SparseCore 0:
  73.6 40.8 all-gather.6
  119.9 36.8 all-gather.8
  239.2 105.1 all-reduce.1
where the time goes:
time: 355 us; the launch traced here: 352 us
  waiting for transfers between devices  129 us (36%)
  other arithmetic  53.6 us (15%)
  matrix products  47.3 us (13%)
  local copies, waits for them, and re-layouts  41.7 us (12%)
  blocking collectives  36.6 us (10%)
  loops' own time  22.3 us (6%)
  between operations  14 us (4%)
  starting transfers between devices  7.71 us (2%)
    psum x1, waiting for transfers between devices, from_root(): return lax.psum(kept, axis)  101 us
    dot_general x32, matrix products, mix(): return jnp.einsum(form, left, right, precision=lax.Precision.HIGHEST)  44.2 us
    all_gather x1, blocking collectives, entering(): lax.all_gather(part.astype(kind), axis)  22.3 us
    all_gather x1, waiting for transfers between devices, entering_2(): gathered = jax.tree.map(lambda a: lax.all_gather(a, axis), part)  17.6 us
    select_n x16, other arithmetic, turn(): return jax.tree.map(lambda a, b: jnp.where(reached, a, b), new, before)  16.3 us
    add x14, other arithmetic, merge_decayed_states(): jnp.exp2(later[0])[:, None, None] * earlier[1] + later[1]  14.9 us
    all_gather x1, blocking collectives, entering_2(): gathered = jax.tree.map(lambda a: lax.all_gather(a, axis), part)  14.3 us
    dynamic_slice x16, local copies, waits for them, and re-layouts, pieces(): lax.dynamic_index_in_dim(whole, index, 0, keepdims=False)  11.1 us
  transfers between devices with their start and end apart: 4, of which 3 were waited for; matrix products, arithmetic and copies ran while one was open for 11% of the time, Pallas kernels for 0%

commit v1 on v0

v1 whole, which is shorter than its diff:
```python
import functools

import jax
import jax.numpy as jnp
from jax import lax
from jax.experimental import pallas as pl
from jax.experimental.pallas import tpu as pltpu
from jax.sharding import PartitionSpec as P

D = 128
C = 256
MESH = pl.DeviceIdType.MESH
F32 = jnp.float32
BF16 = jnp.bfloat16
NN = ((1,), (0,))
NT = ((1,), (1,))


def dot(a, b, dims):
    return lax.dot_general(a, b, (dims, ((), ())), preferred_element_type=F32)


def far(step, size):
    return min(step, size - step)


def layer(
    sizes,
    q_hbm, k_hbm, v_hbm, og_hbm, st_hbm, exps, bnds,
    dq_ref, dk_ref, dv_ref, sg_ref,
    q, k, v, g, st, ncol, nrow, tail, hin, w, wt, pk, qh,
    dqi, dki, dvi, prevs, nexts, edge_state,
    fs, fr, fo, fin, fins, bs, br, bo, bin_, bins,
    lsem, gs, gr, fsem, bsem,
):
    heads, chunks, tokens, segments, nbounds, total = sizes
    groups = 16
    ctx = lax.axis_index("ctx")
    me = lax.axis_index("head")
    z, core = ctx // 2, ctx % 2
    y, x = me // 4, me % 4
    rows_each = tokens // groups
    width = heads * D
    srow = D // segments

    head_steps = sorted(
        [(a, b) for a in range(4) for b in range(4) if a or b],
        key=lambda s: -(far(s[0], 4) + far(s[1], 4)),
    )
    ctx_steps = sorted(
        [(a, b) for a in range(segments // 2) for b in range(2) if a or b],
        key=lambda s: -far(s[0], segments // 2),
    )

    def head_peer(step):
        return lax.rem(y + step[0], 4) * 4 + lax.rem(x + step[1], 4)

    def ctx_peer(step):
        return lax.rem(z + step[0], segments // 2) * 2 + lax.rem(core + step[1], 2)

    barrier = pltpu.get_barrier_semaphore()
    for s in head_steps:
        pl.semaphore_signal(barrier, inc=1, device_id=(ctx, head_peer(s)), device_id_type=MESH)
    for s in ctx_steps:
        pl.semaphore_signal(barrier, inc=1, device_id=(ctx_peer(s), me), device_id_type=MESH)

    loads = [
        pltpu.make_async_copy(k_hbm, k, lsem.at[0]),
        pltpu.make_async_copy(v_hbm, v, lsem.at[1]),
        pltpu.make_async_copy(q_hbm, q, lsem.at[2]),
        pltpu.make_async_copy(st_hbm.at[:, pl.ds(pl.multiple_of(ctx * srow, srow), srow), :], st, lsem.at[3]),
    ]
    for c in loads:
        c.start()

    start = ctx * tokens

    def count(t):
        n = jnp.int32(0)
        for b in range(nbounds):
            n = n + jnp.where(bnds[b] <= t, 1, 0)
        return n.astype(F32)

    def rate(h):
        return exps[h].astype(F32) * (1.0 / (4.0 * total))

    def row(value):
        return jnp.exp2(jnp.full((1, D), value, F32))

    def counts(c, _):
        first = start + c * C
        tc = first + lax.broadcasted_iota(jnp.int32, (C, D), 0)
        tr = first + lax.broadcasted_iota(jnp.int32, (8, C), 1)
        nc = jnp.zeros((C, D), F32)
        nr = jnp.zeros((8, C), F32)
        for b in range(nbounds):
            nc = nc + jnp.where(tc >= bnds[b], 1.0, 0.0)
            nr = nr + jnp.where(tr >= bnds[b], 1.0, 0.0)
        ncol[pl.ds(pl.multiple_of(c * C, C), C), :] = nc
        nrow[c] = nr
        return 0

    lax.fori_loop(0, chunks, counts, 0)

    def rates(i, _):
        h, c = i // chunks, lax.rem(i, chunks)
        at = pl.ds(pl.multiple_of(c * C, C), C)
        a = rate(h)
        n = ncol[at, :]
        place = lax.broadcasted_iota(jnp.int32, (C, D), 0).astype(F32)
        before = count(start + c * C - 1)
        after = count(start + c * C + C - 1)
        hin[h, at, :] = jnp.exp2(-a * (place + 1.0) - (n - before))
        tail[h, at, :] = jnp.exp2(-a * ((C - 1.0) - place) - (after - n))
        return 0

    lax.fori_loop(0, heads * chunks, rates, 0)

    pl.semaphore_wait(barrier, len(head_steps) + len(ctx_steps))

    mine = pl.ds(pl.multiple_of(me * rows_each, rows_each), rows_each)
    for h in range(heads):
        at = pl.multiple_of(me * width + h * D, D)
        pltpu.make_async_copy(og_hbm.at[:, pl.ds(at, D)], g.at[mine, pl.ds(h * D, D)], gr.at[h]).start()

    def send_head(h, _):
        for s in head_steps:
            peer = head_peer(s)
            at = pl.multiple_of(peer * width + h * D, D)
            pltpu.make_async_remote_copy(
                src_ref=og_hbm.at[:, pl.ds(at, D)],
                dst_ref=g.at[mine, pl.ds(pl.multiple_of(h * D, D), D)],
                send_sem=gs,
                recv_sem=gr.at[h],
                device_id=(ctx, peer),
                device_id_type=MESH,
            ).start()
        return 0

    lax.fori_loop(0, heads, send_head, 0)

    def exchange(src, dst, ssem, rsem):
        for s in ctx_steps:
            peer = ctx_peer(s)
            pltpu.make_async_remote_copy(
                src_ref=src.at[peer],
                dst_ref=dst.at[ctx],
                send_sem=ssem,
                recv_sem=rsem,
                device_id=(peer, me),
                device_id_type=MESH,
            ).start()
        dst[ctx] = src[ctx]

    def arrived(buf, sem):
        part = buf.at[pl.ds(0, segments - 1)]
        pltpu.make_async_copy(part, part, sem).wait()

    def seg_decay(lo, hi, d):
        a = jnp.concatenate([jnp.full((srow, D), rate(h), F32) for h in range(lo, hi)], axis=0)
        hits = count((d + 1) * tokens - 1) - count(d * tokens - 1)
        return jnp.exp2(-a * float(tokens) - hits)

    def last(h, c):
        hits = count(start + c * C + C - 1) - count(start + c * C - 1)
        return row(-rate(h) * float(C) - hits)

    loads[0].wait()
    loads[1].wait()

    def own_forward(h, _):
        lanes = pl.ds(pl.multiple_of(h * D, D), D)

        def one(c, s):
            at = pl.ds(pl.multiple_of(c * C, C), C)
            kt = (k[at, lanes].astype(F32) * tail[h, at, :]).T.astype(BF16)
            prevs[h, c] = s
            return last(h, c) * s + dot(kt, v[at, lanes], NN)

        edge_state[h] = lax.fori_loop(0, chunks, one, jnp.zeros((D, D), F32))
        return 0

    lax.fori_loop(0, heads, own_forward, 0)

    def stage_forward(j, _):
        at = pl.ds(pl.multiple_of(j * srow, srow), srow)
        fs[j] = edge_state[:, at, :].reshape(heads * srow, D).astype(BF16)
        return 0

    lax.fori_loop(0, segments, stage_forward, 0)
    exchange(fs, fr, fsem.at[0], fsem.at[1])

    loads[2].wait()
    loads[3].wait()

    def prepare(i, _):
        h, c = i // chunks, lax.rem(i, chunks)
        at = pl.ds(pl.multiple_of(c * C, C), C)
        lanes = pl.ds(pl.multiple_of(h * D, D), D)
        a = rate(h)
        n = ncol[at, :]
        nc = jnp.concatenate([n, n], axis=1)
        nr = nrow[c][0:1, :]
        gap = (
            lax.broadcasted_iota(jnp.int32, (C, C), 0) - lax.broadcasted_iota(jnp.int32, (C, C), 1)
        ).astype(F32)
        dn = nc - nr
        w[i] = jnp.where(gap >= 0, jnp.exp2(-a * gap - dn), 0.0)
        weight = jnp.where(gap <= 0, jnp.exp2(a * gap + dn), 0.0)
        wt[i] = weight
        qc = q[at, lanes]
        pk[i] = (dot(k[at, lanes], qc, NT) * weight).astype(BF16)
        qh[i] = (qc.astype(F32) * hin[h, at, :]).T.astype(BF16)
        return 0

    lax.fori_loop(0, heads * chunks, prepare, 0)

    def own_backward(h):
        lanes = pl.ds(h * D, D)
        col = g.at[:, lanes]
        pltpu.make_async_copy(col, col, gr.at[h]).wait()

        def one(i, s):
            c = chunks - 1 - i
            at = pl.ds(pl.multiple_of(c * C, C), C)
            nexts[h, c] = s
            return last(h, c) * s + dot(qh[h * chunks + c], g[at, lanes], NN)

        edge_state[h] = lax.fori_loop(0, chunks, one, jnp.zeros((D, D), F32))

    def send_backward(p):
        def stage(j, _):
            at = pl.ds(pl.multiple_of(j * srow, srow), srow)
            bs[p, j] = edge_state[pl.ds(2 * p, 2), at, :].reshape(2 * srow, D).astype(BF16)
            return 0

        lax.fori_loop(0, segments, stage, 0)
        exchange(bs.at[p], br.at[p], bsem.at[p, 0], bsem.at[p, 1])

    def scan_forward():
        arrived(fr, fsem.at[1])

        def one(d, s):
            fo[d] = s.astype(BF16)
            return seg_decay(0, heads, d) * s + fr[d].astype(F32)

        lax.fori_loop(0, segments, one, st[...].reshape(heads * srow, D))
        exchange(fo, fin, fsem.at[2], fsem.at[3])

    def scan_backward(p):
        arrived(br.at[p], bsem.at[p, 1])

        def one(i, s):
            d = segments - 1 - i
            bo[p, d] = s.astype(BF16)
            return seg_decay(2 * p, 2 * p + 2, d) * s + br[p, d].astype(F32)

        whole = lax.fori_loop(0, segments, one, jnp.zeros((2 * srow, D), F32))
        sg_ref[pl.ds(2 * p, 2)] = whole.reshape(2, srow, D)
        exchange(bo.at[p], bin_.at[p], bsem.at[p, 2], bsem.at[p, 3])

    def inside(h):
        lanes = pl.ds(h * D, D)

        def one(c, _):
            at = pl.ds(pl.multiple_of(c * C, C), C)
            i = h * chunks + c
            gc, vc = g[at, lanes], v[at, lanes]
            grad = (dot(gc, vc, NT) * w[i]).astype(BF16)
            dqi[at, lanes] = dot(grad, k[at, lanes], NN)
            turned = (dot(vc, gc, NT) * wt[i]).astype(BF16)
            dki[at, lanes] = dot(turned, q[at, lanes], NN)
            dvi[at, lanes] = dot(pk[i], gc, NN)
            return 0

        lax.fori_loop(0, chunks, one, 0)

    def finish_query():
        arrived(fin, fsem.at[3])
        got = fin[...].astype(F32)
        for h in range(heads):
            fins[h] = got[:, h * srow:(h + 1) * srow, :].reshape(D, D)

        def one(i, _):
            h, c = i // chunks, lax.rem(i, chunks)
            at = pl.ds(pl.multiple_of(c * C, C), C)
            lanes = pl.ds(pl.multiple_of(h * D, D), D)
            hits = count(start + c * C - 1) - count(start - 1)
            reach = row(-rate(h) * (c * C).astype(F32) - hits)
            state = (prevs[h, c] + reach * fins[h]).astype(BF16)
            dq_ref[at, lanes] = (dqi[at, lanes] + hin[h, at, :] * dot(g[at, lanes], state, NT)).astype(BF16)
            return 0

        lax.fori_loop(0, heads * chunks, one, 0)

    def finish_keys(p):
        arrived(bin_.at[p], bsem.at[p, 3])
        got = bin_[p].astype(F32)
        for e in range(2):
            bins[2 * p + e] = got[:, e * srow:(e + 1) * srow, :].reshape(D, D)

        def one(i, _):
            h, c = 2 * p + i // chunks, lax.rem(i, chunks)
            at = pl.ds(pl.multiple_of(c * C, C), C)
            lanes = pl.ds(pl.multiple_of(h * D, D), D)
            hits = count(start + tokens - 1) - count(start + c * C + C - 1)
            reach = row(-rate(h) * (tokens - C - c * C).astype(F32) - hits)
            grad = (nexts[h, c] + reach * bins[h]).astype(BF16)
            scale = tail[h, at, :]
            dk_ref[at, lanes] = (dki[at, lanes] + scale * dot(v[at, lanes], grad, NT)).astype(BF16)
            dv_ref[at, lanes] = (dvi[at, lanes] + scale * dot(k[at, lanes], grad, NN)).astype(BF16)
            return 0

        lax.fori_loop(0, 2 * chunks, one, 0)

    own_backward(0)
    own_backward(1)
    send_backward(0)
    scan_forward()
    inside(0)
    own_backward(2)
    own_backward(3)
    send_backward(1)
    scan_backward(0)
    inside(1)
    inside(2)
    scan_backward(1)
    inside(3)
    finish_query()
    finish_keys(0)
    finish_keys(1)

    sent = og_hbm.at[:, pl.ds(0, (groups - 1) * width)]
    pltpu.make_async_copy(sent, sent, gs).wait()
    arrived(fs, fsem.at[0])
    arrived(fo, fsem.at[2])
    for p in range(heads // 2):
        arrived(bs.at[p], bsem.at[p, 0])
        arrived(bo.at[p], bsem.at[p, 2])


def store(a, b, c, s, oa, ob, oc, os, sem):
    rows = a.shape[0] // 4
    copies = [pltpu.make_async_copy(s, os, sem.at[12])]
    for i in range(4):
        at = pl.ds(i * rows, rows)
        for j, (src, dst) in enumerate(((a, oa), (b, ob), (c, oc))):
            copies.append(pltpu.make_async_copy(src.at[at], dst.at[at], sem.at[3 * i + j]))
    for copy in copies:
        copy.start()
    for copy in copies:
        copy.wait()


def shards(queries, keys, values, out_grad, state_in, exponents, boundaries):
    tokens, width = queries.shape
    heads = width // D
    chunks = tokens // C
    segments = lax.axis_size("ctx")
    srow = D // segments
    total = tokens * segments
    sizes = (heads, chunks, tokens, segments, boundaries.shape[0], total)
    hbm = pl.BlockSpec(memory_space=pltpu.HBM)
    vmem = pl.BlockSpec(memory_space=pltpu.VMEM)
    smem = pl.BlockSpec(memory_space=pltpu.SMEM)
    n = heads * chunks
    slab = lambda rows: pltpu.VMEM((segments, rows, D), BF16)
    pair = lambda: pltpu.VMEM((heads // 2, segments, 2 * srow, D), BF16)
    results = pl.pallas_call(
        functools.partial(layer, sizes),
        name="layer",
        out_shape=(
            pltpu.VMEM((tokens, width), BF16),
            pltpu.VMEM((tokens, width), BF16),
            pltpu.VMEM((tokens, width), BF16),
            pltpu.VMEM((heads, srow, D), F32),
        ),
        in_specs=[hbm] * 5 + [smem] * 2,
        out_specs=(vmem,) * 4,
        scratch_shapes=[
            pltpu.VMEM((tokens, width), BF16),
            pltpu.VMEM((tokens, width), BF16),
            pltpu.VMEM((tokens, width), BF16),
            pltpu.VMEM((tokens, width), BF16),
            pltpu.VMEM((heads, srow, D), F32),
            pltpu.VMEM((tokens, D), F32),
            pltpu.VMEM((chunks, 8, C), F32),
            pltpu.VMEM((heads, tokens, D), F32),
            pltpu.VMEM((heads, tokens, D), F32),
            pltpu.VMEM((n, C, C), F32),
            pltpu.VMEM((n, C, C), F32),
            pltpu.VMEM((n, C, C), BF16),
            pltpu.VMEM((n, D, C), BF16),
            pltpu.VMEM((tokens, width), F32),
            pltpu.VMEM((tokens, width), F32),
            pltpu.VMEM((tokens, width), F32),
            pltpu.VMEM((heads, chunks, D, D), F32),
            pltpu.VMEM((heads, chunks, D, D), F32),
            pltpu.VMEM((heads, D, D), F32),
            slab(heads * srow),
            slab(heads * srow),
            slab(heads * srow),
            slab(heads * srow),
            pltpu.VMEM((heads, D, D), F32),
            pair(),
            pair(),
            pair(),
            pair(),
            pltpu.VMEM((heads, D, D), F32),
            pltpu.SemaphoreType.DMA((4,)),
            pltpu.SemaphoreType.DMA,
            pltpu.SemaphoreType.DMA((heads,)),
            pltpu.SemaphoreType.DMA((4,)),
            pltpu.SemaphoreType.DMA((heads // 2, 4)),
        ],
        compiler_params=pltpu.CompilerParams(
            collective_id=0, has_side_effects=True, vmem_limit_bytes=48 << 20
        ),
    )(queries, keys, values, out_grad, state_in, exponents, boundaries)
    whole = jax.ShapeDtypeStruct((tokens, width), BF16)
    return pl.pallas_call(
        store,
        name="store",
        out_shape=(whole, whole, whole, jax.ShapeDtypeStruct((heads, srow, D), F32)),
        in_specs=[vmem] * 4,
        out_specs=(hbm,) * 4,
        scratch_shapes=[pltpu.SemaphoreType.DMA((13,))],
    )(*results)


def solution(mesh):
    in_specs = (
        P("ctx", "head"),
        P("ctx", "head"),
        P("ctx", "head"),
        P(("ctx", "head"), None),
        P("head", None, None),
        P("head"),
        P(),
    )
    out_specs = (P("ctx", "head"), P("ctx", "head"), P("ctx", "head"), P("head", "ctx", None))
    return jax.shard_map(shards, mesh=mesh, in_specs=in_specs, out_specs=out_specs, check_vma=False)
```

time: 355 us -> 53.5 us (0.15)
  waiting for transfers between devices: 129 us -> 0 us
  other arithmetic: 53.6 us -> 0 us
  matrix products: 47.3 us -> 0 us
  Pallas kernels: 0 us -> 44.4 us
  blocking collectives: 36.6 us -> 0 us
  local copies, waits for them, and re-layouts: 41.7 us -> 8.25 us
  loops' own time: 22.3 us -> 0 us
  between operations: 14 us -> 0.67 us
  starting transfers between devices: 7.71 us -> 0 us
    psum x1 -> x0, waiting for transfers between devices: 101 us -> none  [from_root(): return lax.psum(kept, axis)]
    dot_general x40 -> x0, matrix products: 47.3 us -> none  [the longest x32 44.2 us: mix(): return jnp.einsum(form, left, right, precision=lax.Precision.HIGHEST)]
    pallas_call x0 -> x2, Pallas kernels: none -> 44.4 us  [the longest x1 40.8 us: shards(): pl.pallas_call(functools.partial(layer, sizes), name='layer', out_shape=(...]
    all_gather x2 -> x0, blocking collectives: 36.6 us -> none  [the longest x1 22.3 us: entering(): lax.all_gather(part.astype(kind), axis)]
    add x41 -> x0, other arithmetic: 26.6 us -> none  [the longest x14 14.9 us: merge_decayed_states(): jnp.exp2(later[0])[:, None, None] * earlier[1] + later[1]]
    another operation x6 -> x0, loops' own time: 22.3 us -> none  [the longest x1 10.6 us: shards(): lax.scan(own_terms, None, indices)]
    all_gather x2 -> x0, waiting for transfers between devices: 17.6 us -> none  [the longest x1 17.6 us: entering_2(): gathered = jax.tree.map(lambda a: lax.all_gather(a, axis), part)]
    dynamic_slice x25 -> x0, local copies, waits for them, and re-layouts: 17.3 us -> none  [the longest x16 11.1 us: pieces(): lax.dynamic_index_in_dim(whole, index, 0, keepdims=False)]
  transfers between devices with their start and end apart: 4 -> 0, of which waited for: 3 -> 0; matrix products, arithmetic and copies ran while one was open for 11% -> 0% of each run, Pallas kernels for 0% -> 0%
where the time goes in v1:
time: 53.5 us; the launch traced here: 53.3 us
  Pallas kernels  44.4 us (83%)
  local copies, waits for them, and re-layouts  8.25 us (15%)
  between operations  0.67 us (1%)
    pallas_call x1, Pallas kernels, shards(): pl.pallas_call(functools.partial(layer, sizes), name='layer', out_shape=(...  40.8 us
    unnamed x18, local copies, waits for them, and re-layouts  8.25 us
    pallas_call x1, Pallas kernels, shards(): pl.pallas_call(store, name='store', out_shape=(whole, whole, whole, jax.S...  3.62 us

profile of v1, /device:TPU:1, one launch (start us, length us, event | category | flops | bytes accessed | tf_op | source)
XLA Modules:
  0.0 53.3 jit_solution(5616678588705053267)
XLA Ops:
  0.6 0.0 copy-start
  0.6 1.2 %copy-done = bf16[1024,512]{1,0:T(8,128)(2,1)S(1)} copy-done((bf16[1024,512]{1,0:T(8,128)(2,1)S(1)}, bf16[1024,512]{1,0:T(8,128)(2,1)}, u32[]{:S(2)}) %copy-start) | copy-done | bytes 1048600
  1.9 0.0 copy-start.1
  1.9 1.2 %copy-done.1 = bf16[1024,512]{1,0:T(8,128)(2,1)S(1)} copy-done((bf16[1024,512]{1,0:T(8,128)(2,1)S(1)}, bf16[1024,512]{1,0:T(8,128)(2,1)}, u32[]{:S(2)}) %copy-start.1) | copy-done | bytes 1048600
  3.1 0.0 copy-start.5
  3.1 0.9 %copy-done.5 = f32[4,128,128]{2,1,0:T(8,128)S(1)} copy-done((f32[4,128,128]{2,1,0:T(8,128)S(1)}, f32[4,128,128]{2,1,0:T(8,128)}, u32[]{:S(2)}) %copy-start.5) | copy-done | bytes 262168
  4.0 0.0 copy-start.7
  4.0 0.7 %copy-done.7 = s32[4]{0:T(128)S(1)} copy-done((s32[4]{0:T(128)S(1)}, s32[4]{0:T(128)}, u32[]{:S(2)}) %copy-start.7) | copy-done | bytes 40
  4.7 0.0 copy-start.8
  4.7 0.7 %copy-done.8 = s32[8]{0:T(128)S(1)} copy-done((s32[8]{0:T(128)S(1)}, s32[8]{0:T(128)}, u32[]{:S(2)}) %copy-start.8) | copy-done | bytes 56
  5.3 40.8 %layer.1 = (bf16[1024,512]{1,0:T(8,128)(2,1)S(1)}, bf16[1024,512]{1,0:T(8,128)(2,1)S(1)}, bf16[1024,512]{1,0:T(8,128)(2,1)S(1)}, f32[4,8,128]{2,1,0:T(8,128)S(1)}) custom-call(bf16[1024,512]{1,0:T(8,128)(2,1)S(1)} %copy-done, bf16[1024,512]{1,0:T(8,128)(2,1)S(1)} %copy-done.1, bf16[1024,512]{1,0:T(8,128)(2,1)} %v_hbm.1, bf16[64,8192]{1,0:T(8,128)(2,1)} %og_hbm.1, ...), custom_call_target="tpu_custom_call" | custom-call | tf_op jit(solution)/shard_map/layer/pallas_call | solution.py:369
  46.1 0.0 copy-start.2
  46.1 1.0 %copy-done.2 = bf16[1024,512]{1,0:T(8,128)(2,1)} copy-done((bf16[1024,512]{1,0:T(8,128)(2,1)}, bf16[1024,512]{1,0:T(8,128)(2,1)S(1)}, u32[]{:S(2)}) %copy-start.2) | copy-done | bytes 1048600
  47.1 0.0 copy-start.3
  47.1 1.0 %copy-done.3 = bf16[1024,512]{1,0:T(8,128)(2,1)} copy-done((bf16[1024,512]{1,0:T(8,128)(2,1)}, bf16[1024,512]{1,0:T(8,128)(2,1)S(1)}, u32[]{:S(2)}) %copy-start.3) | copy-done | bytes 1048600
  48.1 0.0 copy-start.4
  48.1 1.0 %copy-done.4 = bf16[1024,512]{1,0:T(8,128)(2,1)} copy-done((bf16[1024,512]{1,0:T(8,128)(2,1)}, bf16[1024,512]{1,0:T(8,128)(2,1)S(1)}, u32[]{:S(2)}) %copy-start.4) | copy-done | bytes 1048600
  49.1 0.0 copy-start.6
  49.1 0.6 %copy-done.6 = f32[4,8,128]{2,1,0:T(8,128)} copy-done((f32[4,8,128]{2,1,0:T(8,128)}, f32[4,8,128]{2,1,0:T(8,128)S(1)}, u32[]{:S(2)}) %copy-start.6) | copy-done | bytes 16408
  49.7 3.6 %store.1 = (bf16[1024,512]{1,0:T(8,128)(2,1)}, bf16[1024,512]{1,0:T(8,128)(2,1)}, bf16[1024,512]{1,0:T(8,128)(2,1)}, f32[4,8,128]{2,1,0:T(8,128)}) custom-call(bf16[1024,512]{1,0:T(8,128)(2,1)} %copy-done.2, bf16[1024,512]{1,0:T(8,128)(2,1)} %copy-done.3, bf16[1024,512]{1,0:T(8,128)(2,1)} %copy-done.4, f32[4,8,128]{2,1,0:T(8,128)} %copy-done.6), custom_call_target="tpu_custom_call" | custom-call | tf_op jit(solution)/shard_map/store/pallas_call | solution.py:421
Async XLA Ops:
  0.6 1.2 %copy-start = (bf16[1024,512]{1,0:T(8,128)(2,1)S(1)}, bf16[1024,512]{1,0:T(8,128)(2,1)}, u32[]{:S(2)}) copy-start(bf16[1024,512]{1,0:T(8,128)(2,1)} %q_hbm.1) | copy-start | bytes 3145732
  1.9 1.2 %copy-start.1 = (bf16[1024,512]{1,0:T(8,128)(2,1)S(1)}, bf16[1024,512]{1,0:T(8,128)(2,1)}, u32[]{:S(2)}) copy-start(bf16[1024,512]{1,0:T(8,128)(2,1)} %k_hbm.1) | copy-start | bytes 3145732
  3.1 0.9 %copy-start.5 = (f32[4,128,128]{2,1,0:T(8,128)S(1)}, f32[4,128,128]{2,1,0:T(8,128)}, u32[]{:S(2)}) copy-start(f32[4,128,128]{2,1,0:T(8,128)} %st_hbm.1) | copy-start | bytes 786436
  4.0 0.7 %copy-start.7 = (s32[4]{0:T(128)S(1)}, s32[4]{0:T(128)}, u32[]{:S(2)}) copy-start(s32[4]{0:T(128)} %exps.1) | copy-start | bytes 52
  4.7 0.7 %copy-start.8 = (s32[8]{0:T(128)S(1)}, s32[8]{0:T(128)}, u32[]{:S(2)}) copy-start(s32[8]{0:T(128)} %bnds.1) | copy-start | bytes 100
  46.1 1.0 %copy-start.2 = (bf16[1024,512]{1,0:T(8,128)(2,1)}, bf16[1024,512]{1,0:T(8,128)(2,1)S(1)}, u32[]{:S(2)}) copy-start(bf16[1024,512]{1,0:T(8,128)(2,1)S(1)} %get-tuple-element.8.a) | copy-start | bytes 3145732
  47.1 1.0 %copy-start.3 = (bf16[1024,512]{1,0:T(8,128)(2,1)}, bf16[1024,512]{1,0:T(8,128)(2,1)S(1)}, u32[]{:S(2)}) copy-start(bf16[1024,512]{1,0:T(8,128)(2,1)S(1)} %get-tuple-element.9.b) | copy-start | bytes 3145732
  48.1 1.0 %copy-start.4 = (bf16[1024,512]{1,0:T(8,128)(2,1)}, bf16[1024,512]{1,0:T(8,128)(2,1)S(1)}, u32[]{:S(2)}) copy-start(bf16[1024,512]{1,0:T(8,128)(2,1)S(1)} %get-tuple-element.10.c) | copy-start | bytes 3145732
  49.1 0.6 %copy-start.6 = (f32[4,8,128]{2,1,0:T(8,128)}, f32[4,8,128]{2,1,0:T(8,128)S(1)}, u32[]{:S(2)}) copy-start(f32[4,8,128]{2,1,0:T(8,128)S(1)} %get-tuple-element.11.s) | copy-start | bytes 49156

commit v2 on v1

--- a/solution.py
+++ b/solution.py
@@ -177,10 +177,10 @@
             prevs[h, c] = s
             return last(h, c) * s + dot(kt, v[at, lanes], NN)
 
-        edge_state[h] = lax.fori_loop(0, chunks, one, jnp.zeros((D, D), F32))
-        return 0
-
-    lax.fori_loop(0, heads, own_forward, 0)
+        edge_state[h] = lax.fori_loop(0, chunks, one, jnp.zeros((D, D), F32), unroll=True)
+        return 0
+
+    lax.fori_loop(0, heads, own_forward, 0, unroll=True)
 
     def stage_forward(j, _):
         at = pl.ds(pl.multiple_of(j * srow, srow), srow)
@@ -213,7 +213,7 @@
         qh[i] = (qc.astype(F32) * hin[h, at, :]).T.astype(BF16)
         return 0
 
-    lax.fori_loop(0, heads * chunks, prepare, 0)
+    lax.fori_loop(0, heads * chunks, prepare, 0, unroll=True)
 
     def own_backward(h):
         lanes = pl.ds(h * D, D)
@@ -226,7 +226,7 @@
             nexts[h, c] = s
             return last(h, c) * s + dot(qh[h * chunks + c], g[at, lanes], NN)
 
-        edge_state[h] = lax.fori_loop(0, chunks, one, jnp.zeros((D, D), F32))
+        edge_state[h] = lax.fori_loop(0, chunks, one, jnp.zeros((D, D), F32), unroll=True)
 
     def send_backward(p):
         def stage(j, _):
@@ -244,7 +244,7 @@
             fo[d] = s.astype(BF16)
             return seg_decay(0, heads, d) * s + fr[d].astype(F32)
 
-        lax.fori_loop(0, segments, one, st[...].reshape(heads * srow, D))
+        lax.fori_loop(0, segments, one, st[...].reshape(heads * srow, D), unroll=True)
         exchange(fo, fin, fsem.at[2], fsem.at[3])
 
     def scan_backward(p):
@@ -255,7 +255,7 @@
             bo[p, d] = s.astype(BF16)
             return seg_decay(2 * p, 2 * p + 2, d) * s + br[p, d].astype(F32)
 
-        whole = lax.fori_loop(0, segments, one, jnp.zeros((2 * srow, D), F32))
+        whole = lax.fori_loop(0, segments, one, jnp.zeros((2 * srow, D), F32), unroll=True)
         sg_ref[pl.ds(2 * p, 2)] = whole.reshape(2, srow, D)
         exchange(bo.at[p], bin_.at[p], bsem.at[p, 2], bsem.at[p, 3])
 
@@ -273,7 +273,7 @@
             dvi[at, lanes] = dot(pk[i], gc, NN)
             return 0
 
-        lax.fori_loop(0, chunks, one, 0)
+        lax.fori_loop(0, chunks, one, 0, unroll=True)
 
     def finish_query():
         arrived(fin, fsem.at[3])
@@ -291,7 +291,7 @@
             dq_ref[at, lanes] = (dqi[at, lanes] + hin[h, at, :] * dot(g[at, lanes], state, NT)).astype(BF16)
             return 0
 
-        lax.fori_loop(0, heads * chunks, one, 0)
+        lax.fori_loop(0, heads * chunks, one, 0, unroll=True)
 
     def finish_keys(p):
         arrived(bin_.at[p], bsem.at[p, 3])
@@ -311,7 +311,7 @@
             dv_ref[at, lanes] = (dvi[at, lanes] + scale * dot(k[at, lanes], grad, NN)).astype(BF16)
             return 0
 
-        lax.fori_loop(0, 2 * chunks, one, 0)
+        lax.fori_loop(0, 2 * chunks, one, 0, unroll=True)
 
     own_backward(0)
     own_backward(1)
@@ -416,7 +416,10 @@
         compiler_params=pltpu.CompilerParams(
             collective_id=0, has_side_effects=True, vmem_limit_bytes=48 << 20
         ),
-    )(queries, keys, values, out_grad, state_in, exponents, boundaries)
+    )(*[
+        pltpu.with_memory_space_constraint(a, pltpu.HBM)
+        for a in (queries, keys, values, out_grad, state_in, exponents, boundaries)
+    ])
     whole = jax.ShapeDtypeStruct((tokens, width), BF16)
     return pl.pallas_call(
         store,
@@ -425,6 +428,7 @@
         in_specs=[vmem] * 4,
         out_specs=(hbm,) * 4,
         scratch_shapes=[pltpu.SemaphoreType.DMA((13,))],
+        compiler_params=pltpu.CompilerParams(vmem_limit_bytes=4 << 20),
     )(*results)
 
 

time: 53.5 us -> 39.4 us (0.74)
  local copies, waits for them, and re-layouts: 8.25 us -> 0 us
  Pallas kernels: 44.4 us -> 38.7 us
    unnamed x18 -> x0, local copies, waits for them, and re-layouts: 8.25 us -> none
    pallas_call x1, Pallas kernels: 40.8 us -> 36.9 us  [shards(): pl.pallas_call(functools.partial(layer, sizes), name='layer', out_shape=(...]
    pallas_call x1, Pallas kernels: 3.62 us -> 1.77 us  [shards(): pl.pallas_call(store, name='store', out_shape=(whole, whole, whole, jax.S...]
where the time goes in v2:
time: 39.4 us; the launch traced here: 39.3 us
  Pallas kernels  38.7 us (98%)
  between operations  0.64 us (2%)
    pallas_call x1, Pallas kernels, shards(): pl.pallas_call(functools.partial(layer, sizes), name='layer', out_shape=(...  36.9 us
    pallas_call x1, Pallas kernels, shards(): pl.pallas_call(store, name='store', out_shape=(whole, whole, whole, jax.S...  1.77 us

profile of v2, /device:TPU:1, one launch (start us, length us, event | category | flops | bytes accessed | tf_op | source)
XLA Modules:
  0.0 39.3 jit_solution(666668497076471172)
XLA Ops:
  0.6 36.9 %layer.1 = (bf16[1024,512]{1,0:T(8,128)(2,1)S(1)}, bf16[1024,512]{1,0:T(8,128)(2,1)S(1)}, bf16[1024,512]{1,0:T(8,128)(2,1)S(1)}, f32[4,8,128]{2,1,0:T(8,128)S(1)}) custom-call(bf16[1024,512]{1,0:T(8,128)(2,1)} %q_hbm.1, bf16[1024,512]{1,0:T(8,128)(2,1)} %k_hbm.1, bf16[1024,512]{1,0:T(8,128)(2,1)} %v_hbm.1, bf16[64,8192]{1,0:T(8,128)(2,1)} %og_hbm.1, ...), custom_call_target="tpu_custom_call" | custom-call | tf_op jit(solution)/shard_map/layer/pallas_call | solution.py:369
  37.6 1.8 %store.1 = (bf16[1024,512]{1,0:T(8,128)(2,1)}, bf16[1024,512]{1,0:T(8,128)(2,1)}, bf16[1024,512]{1,0:T(8,128)(2,1)}, f32[4,8,128]{2,1,0:T(8,128)}) custom-call(bf16[1024,512]{1,0:T(8,128)(2,1)S(1)} %get-tuple-element.8.a, bf16[1024,512]{1,0:T(8,128)(2,1)S(1)} %get-tuple-element.9.b, bf16[1024,512]{1,0:T(8,128)(2,1)S(1)} %get-tuple-element.10.c, ...), custom_call_target="tpu_custom_call" | custom-call | tf_op jit(solution)/shard_map/store/pallas_call | solution.py:424

commit v3 on v2

--- a/solution.py
+++ b/solution.py
@@ -27,11 +27,13 @@
 def layer(
     sizes,
     q_hbm, k_hbm, v_hbm, og_hbm, st_hbm, exps, bnds,
-    dq_ref, dk_ref, dv_ref, sg_ref,
+    dq_ref, dk_ref, dv_ref, sg_ref, ki_ref, vi_ref, kl_ref, vl_ref, scale_ref, grad_ref,
     q, k, v, g, st, ncol, nrow, tail, hin, w, wt, pk, qh,
     dqi, dki, dvi, prevs, nexts, edge_state,
     fs, fr, fo, fin, fins, bs, br, bo, bin_, bins,
-    lsem, gs, gr, fsem, bsem,
+    cs, cr, co, ci, gs_out, gs_in,
+    segd, lastd, befored, afterd,
+    lsem, gs, gr, fsem, bsem, csem, osem, ssem,
 ):
     heads, chunks, tokens, segments, nbounds, total = sizes
     groups = 16
@@ -42,6 +44,7 @@
     rows_each = tokens // groups
     width = heads * D
     srow = D // segments
+    zs = segments // 2
 
     head_steps = sorted(
         [(a, b) for a in range(4) for b in range(4) if a or b],
@@ -84,8 +87,24 @@
     def rate(h):
         return exps[h].astype(F32) * (1.0 / (4.0 * total))
 
-    def row(value):
-        return jnp.exp2(jnp.full((1, D), value, F32))
+    def tile(value):
+        return jnp.exp2(jnp.full((8, D), value, F32))
+
+    def segment_decays(d, _):
+        hits = count((d + 1) * tokens - 1) - count(d * tokens - 1)
+        for h in range(heads):
+            segd[h, d] = tile(-rate(h) * float(tokens) - hits)
+        return 0
+
+    def chunk_decays(c, _):
+        low, high = count(start + c * C - 1), count(start + c * C + C - 1)
+        first, end = count(start - 1), count(start + tokens - 1)
+        passed = (c * C).astype(F32)
+        for h in range(heads):
+            lastd[h, c] = tile(-rate(h) * float(C) - (high - low))
+            befored[h, c] = tile(-rate(h) * passed - (low - first))
+            afterd[h, c] = tile(-rate(h) * (float(tokens - C) - passed) - (end - high))
+        return 0
 
     def counts(c, _):
         first = start + c * C
@@ -100,8 +119,6 @@
         nrow[c] = nr
         return 0
 
-    lax.fori_loop(0, chunks, counts, 0)
-
     def rates(i, _):
         h, c = i // chunks, lax.rem(i, chunks)
         at = pl.ds(pl.multiple_of(c * C, C), C)
@@ -114,15 +131,9 @@
         tail[h, at, :] = jnp.exp2(-a * ((C - 1.0) - place) - (after - n))
         return 0
 
-    lax.fori_loop(0, heads * chunks, rates, 0)
-
     pl.semaphore_wait(barrier, len(head_steps) + len(ctx_steps))
 
     mine = pl.ds(pl.multiple_of(me * rows_each, rows_each), rows_each)
-    for h in range(heads):
-        at = pl.multiple_of(me * width + h * D, D)
-        pltpu.make_async_copy(og_hbm.at[:, pl.ds(at, D)], g.at[mine, pl.ds(h * D, D)], gr.at[h]).start()
-
     def send_head(h, _):
         for s in head_steps:
             peer = head_peer(s)
@@ -138,6 +149,14 @@
         return 0
 
     lax.fori_loop(0, heads, send_head, 0)
+    for h in range(heads):
+        at = pl.multiple_of(me * width + h * D, D)
+        pltpu.make_async_copy(og_hbm.at[:, pl.ds(at, D)], g.at[mine, pl.ds(h * D, D)], gr.at[h]).start()
+
+    lax.fori_loop(0, chunks, counts, 0)
+    lax.fori_loop(0, heads * chunks, rates, 0)
+    lax.fori_loop(0, chunks, chunk_decays, 0)
+    lax.fori_loop(0, segments, segment_decays, 0)
 
     def exchange(src, dst, ssem, rsem):
         for s in ctx_steps:
@@ -157,13 +176,10 @@
         pltpu.make_async_copy(part, part, sem).wait()
 
     def seg_decay(lo, hi, d):
-        a = jnp.concatenate([jnp.full((srow, D), rate(h), F32) for h in range(lo, hi)], axis=0)
-        hits = count((d + 1) * tokens - 1) - count(d * tokens - 1)
-        return jnp.exp2(-a * float(tokens) - hits)
+        return segd[lo:hi, d].reshape((hi - lo) * srow, D)
 
     def last(h, c):
-        hits = count(start + c * C + C - 1) - count(start + c * C - 1)
-        return row(-rate(h) * float(C) - hits)
+        return lastd[h, c, 0:1, :]
 
     loads[0].wait()
     loads[1].wait()
@@ -214,6 +230,9 @@
         return 0
 
     lax.fori_loop(0, heads * chunks, prepare, 0, unroll=True)
+    kl_ref[...] = k[:, (heads - 1) * D:]
+    vl_ref[...] = v[:, (heads - 1) * D:]
+    scale_ref[...] = tail[heads - 1]
 
     def own_backward(h):
         lanes = pl.ds(h * D, D)
@@ -236,6 +255,85 @@
 
         lax.fori_loop(0, segments, stage, 0)
         exchange(bs.at[p], br.at[p], bsem.at[p, 0], bsem.at[p, 1])
+
+    def send_single(e):
+        h = 2 + e
+        cs[e] = edge_state[h].reshape(zs, D // zs, D).astype(BF16)
+
+        def copy(to):
+            return pltpu.make_async_remote_copy(
+                src_ref=cs.at[e, to], dst_ref=cr.at[e, ctx], send_sem=csem.at[e, 0], recv_sem=csem.at[e, 1],
+                device_id=(2 * to + e, me), device_id_type=MESH,
+            )
+
+        for step in sorted(range(1, zs), key=lambda n: -far(n, zs)):
+            copy(lax.rem(z + step, zs)).start()
+
+        @pl.when(core == e)
+        def _():
+            cr[e, ctx] = cs[e, z]
+
+        @pl.when(core != e)
+        def _():
+            copy(z).start()
+
+    def scan_single(e):
+        h = 2 + e
+
+        @pl.when(core == e)
+        def _():
+            arrived(cr.at[e], csem.at[e, 1])
+
+            def one(i, s):
+                d = segments - 1 - i
+                co[d] = s.astype(BF16)
+                return segd[h, d, 0:1, :] * s + cr[e, d].astype(F32)
+
+            whole = lax.fori_loop(0, segments, one, jnp.zeros((D // zs, D), F32), unroll=True)
+            for step in ctx_steps:
+                peer = ctx_peer(step)
+                pltpu.make_async_remote_copy(
+                    src_ref=co.at[peer], dst_ref=ci.at[e, z], send_sem=osem.at[e, 0], recv_sem=osem.at[e, 1],
+                    device_id=(peer, me), device_id_type=MESH,
+                ).start()
+            ci[e, z] = co[ctx]
+            sg_ref[h] = whole[e * srow:(e + 1) * srow, :]
+            gs_out[...] = whole[(1 - e) * srow:(2 - e) * srow, :]
+            swap_rows().start()
+
+    def swap_rows():
+        return pltpu.make_async_remote_copy(
+            src_ref=gs_out, dst_ref=gs_in, send_sem=ssem.at[0], recv_sem=ssem.at[1],
+            device_id=(2 * z + 1 - core, me), device_id_type=MESH,
+        )
+
+    def slots(buf, n, sem):
+        part = buf.at[pl.ds(0, n)]
+        pltpu.make_async_copy(part, part, sem).wait()
+
+    def join_single(e):
+        @pl.when(core == e)
+        def _():
+            slots(ci.at[e], zs - 1, osem.at[e, 1])
+
+        @pl.when(core != e)
+        def _():
+            slots(ci.at[e], zs, osem.at[e, 1])
+
+        bins[2 + e] = ci[e].astype(F32).reshape(D, D)
+
+    def end_single():
+        swap_rows().wait()
+        for e in range(2):
+            @pl.when(core == e)
+            def _():
+                sg_ref[3 - e] = gs_in[...]
+                slots(cs.at[e], zs - 1, csem.at[e, 0])
+                slots(co, segments - 1, osem.at[e, 0])
+
+            @pl.when(core != e)
+            def _():
+                slots(cs.at[e], zs, csem.at[e, 0])
 
     def scan_forward():
         arrived(fr, fsem.at[1])
@@ -269,8 +367,13 @@
             grad = (dot(gc, vc, NT) * w[i]).astype(BF16)
             dqi[at, lanes] = dot(grad, k[at, lanes], NN)
             turned = (dot(vc, gc, NT) * wt[i]).astype(BF16)
-            dki[at, lanes] = dot(turned, q[at, lanes], NN)
-            dvi[at, lanes] = dot(pk[i], gc, NN)
+            dk_part, dv_part = dot(turned, q[at, lanes], NN), dot(pk[i], gc, NN)
+            if h == heads - 1:
+                ki_ref[at, :] = dk_part
+                vi_ref[at, :] = dv_part
+            else:
+                dki[at, lanes] = dk_part
+                dvi[at, lanes] = dv_part
             return 0
 
         lax.fori_loop(0, chunks, one, 0, unroll=True)
@@ -285,69 +388,83 @@
             h, c = i // chunks, lax.rem(i, chunks)
             at = pl.ds(pl.multiple_of(c * C, C), C)
             lanes = pl.ds(pl.multiple_of(h * D, D), D)
-            hits = count(start + c * C - 1) - count(start - 1)
-            reach = row(-rate(h) * (c * C).astype(F32) - hits)
-            state = (prevs[h, c] + reach * fins[h]).astype(BF16)
+            state = (prevs[h, c] + befored[h, c, 0:1, :] * fins[h]).astype(BF16)
             dq_ref[at, lanes] = (dqi[at, lanes] + hin[h, at, :] * dot(g[at, lanes], state, NT)).astype(BF16)
             return 0
 
         lax.fori_loop(0, heads * chunks, one, 0, unroll=True)
 
-    def finish_keys(p):
+    def join_pair(p):
         arrived(bin_.at[p], bsem.at[p, 3])
         got = bin_[p].astype(F32)
         for e in range(2):
             bins[2 * p + e] = got[:, e * srow:(e + 1) * srow, :].reshape(D, D)
 
-        def one(i, _):
-            h, c = 2 * p + i // chunks, lax.rem(i, chunks)
+    def finish_keys(h):
+        lanes = pl.ds(h * D, D)
+
+        def one(c, _):
             at = pl.ds(pl.multiple_of(c * C, C), C)
-            lanes = pl.ds(pl.multiple_of(h * D, D), D)
-            hits = count(start + tokens - 1) - count(start + c * C + C - 1)
-            reach = row(-rate(h) * (tokens - C - c * C).astype(F32) - hits)
-            grad = (nexts[h, c] + reach * bins[h]).astype(BF16)
+            grad = (nexts[h, c] + afterd[h, c, 0:1, :] * bins[h]).astype(BF16)
             scale = tail[h, at, :]
             dk_ref[at, lanes] = (dki[at, lanes] + scale * dot(v[at, lanes], grad, NT)).astype(BF16)
             dv_ref[at, lanes] = (dvi[at, lanes] + scale * dot(k[at, lanes], grad, NN)).astype(BF16)
             return 0
 
-        lax.fori_loop(0, 2 * chunks, one, 0, unroll=True)
+        lax.fori_loop(0, chunks, one, 0, unroll=True)
 
     own_backward(0)
+    inside(0)
     own_backward(1)
     send_backward(0)
     scan_forward()
-    inside(0)
+    inside(1)
     own_backward(2)
+    send_single(0)
+    scan_backward(0)
     own_backward(3)
-    send_backward(1)
-    scan_backward(0)
-    inside(1)
+    send_single(1)
     inside(2)
-    scan_backward(1)
+    scan_single(0)
     inside(3)
+    scan_single(1)
     finish_query()
+    join_pair(0)
     finish_keys(0)
     finish_keys(1)
+    join_single(0)
+    finish_keys(2)
+    join_single(1)
+    for c in range(chunks):
+        grad_ref[c] = (nexts[heads - 1, c] + afterd[heads - 1, c, 0:1, :] * bins[heads - 1]).astype(BF16)
 
     sent = og_hbm.at[:, pl.ds(0, (groups - 1) * width)]
     pltpu.make_async_copy(sent, sent, gs).wait()
     arrived(fs, fsem.at[0])
     arrived(fo, fsem.at[2])
-    for p in range(heads // 2):
-        arrived(bs.at[p], bsem.at[p, 0])
-        arrived(bo.at[p], bsem.at[p, 2])
-
-
-def store(a, b, c, s, oa, ob, oc, os, sem):
-    rows = a.shape[0] // 4
-    copies = [pltpu.make_async_copy(s, os, sem.at[12])]
-    for i in range(4):
-        at = pl.ds(i * rows, rows)
-        for j, (src, dst) in enumerate(((a, oa), (b, ob), (c, oc))):
-            copies.append(pltpu.make_async_copy(src.at[at], dst.at[at], sem.at[3 * i + j]))
+    arrived(bs.at[0], bsem.at[0, 0])
+    arrived(bo.at[0], bsem.at[0, 2])
+    end_single()
+
+
+def store(dq, dk, dv, sg, ki, vi, kl, vl, scale, grad, dq_hbm, dk_hbm, dv_hbm, sg_hbm, lk, lv, sem):
+    rows = dq.shape[0] // 4
+    done = dk.shape[1] - D
+    copies = [pltpu.make_async_copy(dq, dq_hbm, sem.at[0]), pltpu.make_async_copy(sg, sg_hbm, sem.at[1])]
+    for j, (src, dst) in enumerate(((dk, dk_hbm), (dv, dv_hbm))):
+        first = pl.ds(0, done)
+        copies.append(pltpu.make_async_copy(src.at[:, first], dst.at[:, first], sem.at[2 + j]))
     for copy in copies:
         copy.start()
+    for c in range(4):
+        at = pl.ds(c * rows, rows)
+        for j, (part, other, dims, last, dst) in enumerate(
+            ((ki, vl, NT, lk, dk_hbm), (vi, kl, NN, lv, dv_hbm))
+        ):
+            last[at, :] = (part[at, :] + scale[at, :] * dot(other[at, :], grad[c], dims)).astype(BF16)
+            copy = pltpu.make_async_copy(last.at[at], dst.at[at, pl.ds(done, D)], sem.at[4 + 2 * c + j])
+            copy.start()
+            copies.append(copy)
     for copy in copies:
         copy.wait()
 
@@ -365,7 +482,7 @@
     smem = pl.BlockSpec(memory_space=pltpu.SMEM)
     n = heads * chunks
     slab = lambda rows: pltpu.VMEM((segments, rows, D), BF16)
-    pair = lambda: pltpu.VMEM((heads // 2, segments, 2 * srow, D), BF16)
+    pair = lambda: pltpu.VMEM((1, segments, 2 * srow, D), BF16)
     results = pl.pallas_call(
         functools.partial(layer, sizes),
         name="layer",
@@ -374,9 +491,15 @@
             pltpu.VMEM((tokens, width), BF16),
             pltpu.VMEM((tokens, width), BF16),
             pltpu.VMEM((heads, srow, D), F32),
+            pltpu.VMEM((tokens, D), F32),
+            pltpu.VMEM((tokens, D), F32),
+            pltpu.VMEM((tokens, D), BF16),
+            pltpu.VMEM((tokens, D), BF16),
+            pltpu.VMEM((tokens, D), F32),
+            pltpu.VMEM((chunks, D, D), BF16),
         ),
         in_specs=[hbm] * 5 + [smem] * 2,
-        out_specs=(vmem,) * 4,
+        out_specs=(vmem,) * 10,
         scratch_shapes=[
             pltpu.VMEM((tokens, width), BF16),
             pltpu.VMEM((tokens, width), BF16),
@@ -407,11 +530,24 @@
             pair(),
             pair(),
             pltpu.VMEM((heads, D, D), F32),
+            pltpu.VMEM((2, segments // 2, 2 * srow, D), BF16),
+            pltpu.VMEM((2, segments, 2 * srow, D), BF16),
+            pltpu.VMEM((segments, 2 * srow, D), BF16),
+            pltpu.VMEM((2, segments // 2, 2 * srow, D), BF16),
+            pltpu.VMEM((srow, D), F32),
+            pltpu.VMEM((srow, D), F32),
+            pltpu.VMEM((heads, segments, 8, D), F32),
+            pltpu.VMEM((heads, chunks, 8, D), F32),
+            pltpu.VMEM((heads, chunks, 8, D), F32),
+            pltpu.VMEM((heads, chunks, 8, D), F32),
             pltpu.SemaphoreType.DMA((4,)),
             pltpu.SemaphoreType.DMA,
             pltpu.SemaphoreType.DMA((heads,)),
             pltpu.SemaphoreType.DMA((4,)),
-            pltpu.SemaphoreType.DMA((heads // 2, 4)),
+            pltpu.SemaphoreType.DMA((1, 4)),
+            pltpu.SemaphoreType.DMA((2, 2)),
+            pltpu.SemaphoreType.DMA((2, 2)),
+            pltpu.SemaphoreType.DMA((2,)),
         ],
         compiler_params=pltpu.CompilerParams(
             collective_id=0, has_side_effects=True, vmem_limit_bytes=48 << 20
@@ -425,9 +561,13 @@
         store,
         name="store",
         out_shape=(whole, whole, whole, jax.ShapeDtypeStruct((heads, srow, D), F32)),
-        in_specs=[vmem] * 4,
+        in_specs=[vmem] * 10,
         out_specs=(hbm,) * 4,
-        scratch_shapes=[pltpu.SemaphoreType.DMA((13,))],
+        scratch_shapes=[
+            pltpu.VMEM((tokens, D), BF16),
+            pltpu.VMEM((tokens, D), BF16),
+            pltpu.SemaphoreType.DMA((12,)),
+        ],
         compiler_params=pltpu.CompilerParams(vmem_limit_bytes=4 << 20),
     )(*results)
 

time: 39.4 us -> 37.8 us (0.959)
  Pallas kernels: 38.7 us -> 37 us
    pallas_call x1, Pallas kernels: 36.9 us -> 35.3 us  [shards(): pl.pallas_call(functools.partial(layer, sizes), name='layer', out_shape=(...]
where the time goes in v3:
time: 37.8 us; the launch traced here: 37.7 us
  Pallas kernels  37 us (98%)
  between operations  0.64 us (2%)
    pallas_call x1, Pallas kernels, shards(): pl.pallas_call(functools.partial(layer, sizes), name='layer', out_shape=(...  35.3 us
    pallas_call x1, Pallas kernels, shards(): pl.pallas_call(store, name='store', out_shape=(whole, whole, whole, jax.S...  1.76 us

profile of v3, /device:TPU:1, one launch (start us, length us, event | category | flops | bytes accessed | tf_op | source)
XLA Modules:
  0.0 37.7 jit_solution(5067734701032643318)
XLA Ops:
  0.6 35.3 %layer.1 = (bf16[1024,512]{1,0:T(8,128)(2,1)S(1)}, bf16[1024,512]{1,0:T(8,128)(2,1)S(1)}, bf16[1024,512]{1,0:T(8,128)(2,1)S(1)}, f32[4,8,128]{2,1,0:T(8,128)S(1)...) custom-call(bf16[1024,512]{1,0:T(8,128)(2,1)} %q_hbm.1, ...), custom_call_target="tpu_custom_call" | custom-call | tf_op jit(solution)/shard_map/layer/pallas_call | solution.py:486
  35.9 1.8 %store.1 = (bf16[1024,512]{1,0:T(8,128)(2,1)}, bf16[1024,512]{1,0:T(8,128)(2,1)}, bf16[1024,512]{1,0:T(8,128)(2,1)}, f32[4,8,128]{2,1,0:T(8,128)}) custom-call(bf16[1024,512]{1,0:T(8,128)(2,1)S(1)} %get-tuple-element.14.dq, bf16[1024,512]{1,0:T(8,128)(2,1)S(1)} %get-tuple-element.15.dk, bf16[1024,512]{1,0:T(8,128)(2,1)S(1)} %get-tuple-element.16.dv, ...), custom_call_target="tpu_custom_call" | custom-call | tf_op jit(solution)/shard_map/store/pallas_call | solution.py:560

commit v4 on v3

--- a/solution.py
+++ b/solution.py
@@ -26,9 +26,9 @@
 
 def layer(
     sizes,
-    q_hbm, k_hbm, v_hbm, og_hbm, st_hbm, exps, bnds,
+    q_hbm, k_hbm, v_hbm, og_hbm, st_hbm, exps_hbm, bnds_hbm,
     dq_ref, dk_ref, dv_ref, sg_ref, ki_ref, vi_ref, kl_ref, vl_ref, scale_ref, grad_ref,
-    q, k, v, g, st, ncol, nrow, tail, hin, w, wt, pk, qh,
+    exps, bnds, q, k, v, g, st, ncol, nrow, tail, hin, w, wt, pk, qh,
     dqi, dki, dvi, prevs, nexts, edge_state,
     fs, fr, fo, fin, fins, bs, br, bo, bin_, bins,
     cs, cr, co, ci, gs_out, gs_in,
@@ -62,10 +62,10 @@
         return lax.rem(z + step[0], segments // 2) * 2 + lax.rem(core + step[1], 2)
 
     barrier = pltpu.get_barrier_semaphore()
+    for s in ctx_steps:
+        pl.semaphore_signal(barrier, inc=1, device_id=(ctx_peer(s), me), device_id_type=MESH)
     for s in head_steps:
         pl.semaphore_signal(barrier, inc=1, device_id=(ctx, head_peer(s)), device_id_type=MESH)
-    for s in ctx_steps:
-        pl.semaphore_signal(barrier, inc=1, device_id=(ctx_peer(s), me), device_id_type=MESH)
 
     loads = [
         pltpu.make_async_copy(k_hbm, k, lsem.at[0]),
@@ -73,7 +73,11 @@
         pltpu.make_async_copy(q_hbm, q, lsem.at[2]),
         pltpu.make_async_copy(st_hbm.at[:, pl.ds(pl.multiple_of(ctx * srow, srow), srow), :], st, lsem.at[3]),
     ]
-    for c in loads:
+    smalls = [
+        pltpu.make_async_copy(exps_hbm, exps, lsem.at[4]),
+        pltpu.make_async_copy(bnds_hbm, bnds, lsem.at[5]),
+    ]
+    for c in smalls + loads:
         c.start()
 
     start = ctx * tokens
@@ -153,6 +157,8 @@
         at = pl.multiple_of(me * width + h * D, D)
         pltpu.make_async_copy(og_hbm.at[:, pl.ds(at, D)], g.at[mine, pl.ds(h * D, D)], gr.at[h]).start()
 
+    for c in smalls:
+        c.wait()
     lax.fori_loop(0, chunks, counts, 0)
     lax.fori_loop(0, heads * chunks, rates, 0)
     lax.fori_loop(0, chunks, chunk_decays, 0)
@@ -424,8 +430,8 @@
     scan_backward(0)
     own_backward(3)
     send_single(1)
+    scan_single(0)
     inside(2)
-    scan_single(0)
     inside(3)
     scan_single(1)
     finish_query()
@@ -479,7 +485,6 @@
     sizes = (heads, chunks, tokens, segments, boundaries.shape[0], total)
     hbm = pl.BlockSpec(memory_space=pltpu.HBM)
     vmem = pl.BlockSpec(memory_space=pltpu.VMEM)
-    smem = pl.BlockSpec(memory_space=pltpu.SMEM)
     n = heads * chunks
     slab = lambda rows: pltpu.VMEM((segments, rows, D), BF16)
     pair = lambda: pltpu.VMEM((1, segments, 2 * srow, D), BF16)
@@ -498,9 +503,11 @@
             pltpu.VMEM((tokens, D), F32),
             pltpu.VMEM((chunks, D, D), BF16),
         ),
-        in_specs=[hbm] * 5 + [smem] * 2,
+        in_specs=[hbm] * 7,
         out_specs=(vmem,) * 10,
         scratch_shapes=[
+            pltpu.SMEM((heads,), jnp.int32),
+            pltpu.SMEM((boundaries.shape[0],), jnp.int32),
             pltpu.VMEM((tokens, width), BF16),
             pltpu.VMEM((tokens, width), BF16),
             pltpu.VMEM((tokens, width), BF16),
@@ -540,7 +547,7 @@
             pltpu.VMEM((heads, chunks, 8, D), F32),
             pltpu.VMEM((heads, chunks, 8, D), F32),
             pltpu.VMEM((heads, chunks, 8, D), F32),
-            pltpu.SemaphoreType.DMA((4,)),
+            pltpu.SemaphoreType.DMA((6,)),
             pltpu.SemaphoreType.DMA,
             pltpu.SemaphoreType.DMA((heads,)),
             pltpu.SemaphoreType.DMA((4,)),

time: 37.8 us -> 36.8 us (0.974)
  Pallas kernels: 37 us -> 36.1 us
    pallas_call x1, Pallas kernels: 35.3 us -> 34.3 us  [shards(): pl.pallas_call(functools.partial(layer, sizes), name='layer', out_shape=(...]
where the time goes in v4:
time: 36.8 us; the launch traced here: 36.7 us
  Pallas kernels  36.1 us (98%)
  between operations  0.64 us (2%)
    pallas_call x1, Pallas kernels, shards(): pl.pallas_call(functools.partial(layer, sizes), name='layer', out_shape=(...  34.3 us
    pallas_call x1, Pallas kernels, shards(): pl.pallas_call(store, name='store', out_shape=(whole, whole, whole, jax.S...  1.76 us

profile of v4, /device:TPU:1, one launch (start us, length us, event | category | flops | bytes accessed | tf_op | source)
XLA Modules:
  0.0 36.7 jit_solution(6693424486930560023)
XLA Ops:
  0.6 34.3 %layer.1 = (bf16[1024,512]{1,0:T(8,128)(2,1)S(1)}, bf16[1024,512]{1,0:T(8,128)(2,1)S(1)}, bf16[1024,512]{1,0:T(8,128)(2,1)S(1)}, f32[4,8,128]{2,1,0:T(8,128)S(1)...) custom-call(bf16[1024,512]{1,0:T(8,128)(2,1)} %q_hbm.1, ...), custom_call_target="tpu_custom_call" | custom-call | tf_op jit(solution)/shard_map/layer/pallas_call | solution.py:491
  35.0 1.8 %store.1 = (bf16[1024,512]{1,0:T(8,128)(2,1)}, bf16[1024,512]{1,0:T(8,128)(2,1)}, bf16[1024,512]{1,0:T(8,128)(2,1)}, f32[4,8,128]{2,1,0:T(8,128)}) custom-call(bf16[1024,512]{1,0:T(8,128)(2,1)S(1)} %get-tuple-element.14.dq, bf16[1024,512]{1,0:T(8,128)(2,1)S(1)} %get-tuple-element.15.dk, bf16[1024,512]{1,0:T(8,128)(2,1)S(1)} %get-tuple-element.16.dv, ...), custom_call_target="tpu_custom_call" | custom-call | tf_op jit(solution)/shard_map/store/pallas_call | solution.py:567

commit v5 on v4

--- a/solution.py
+++ b/solution.py
@@ -440,10 +440,6 @@
     finish_keys(1)
     join_single(0)
     finish_keys(2)
-    join_single(1)
-    for c in range(chunks):
-        grad_ref[c] = (nexts[heads - 1, c] + afterd[heads - 1, c, 0:1, :] * bins[heads - 1]).astype(BF16)
-
     sent = og_hbm.at[:, pl.ds(0, (groups - 1) * width)]
     pltpu.make_async_copy(sent, sent, gs).wait()
     arrived(fs, fsem.at[0])
@@ -451,6 +447,9 @@
     arrived(bs.at[0], bsem.at[0, 0])
     arrived(bo.at[0], bsem.at[0, 2])
     end_single()
+    join_single(1)
+    for c in range(chunks):
+        grad_ref[c] = (nexts[heads - 1, c] + afterd[heads - 1, c, 0:1, :] * bins[heads - 1]).astype(BF16)
 
 
 def store(dq, dk, dv, sg, ki, vi, kl, vl, scale, grad, dq_hbm, dk_hbm, dv_hbm, sg_hbm, lk, lv, sem):

time: 36.8 us -> 36.8 us (level)
  no operation moved by 1% of the time
where the time goes in v5:
time: 36.8 us; the launch traced here: 36.7 us
  Pallas kernels  36.1 us (98%)
  between operations  0.64 us (2%)
    pallas_call x1, Pallas kernels, shards(): pl.pallas_call(functools.partial(layer, sizes), name='layer', out_shape=(...  34.3 us
    pallas_call x1, Pallas kernels, shards(): pl.pallas_call(store, name='store', out_shape=(whole, whole, whole, jax.S...  1.76 us

profile of v5, /device:TPU:1, one launch (start us, length us, event | category | flops | bytes accessed | tf_op | source)
XLA Modules:
  0.0 36.7 jit_solution(20337963542943919)
XLA Ops:
  0.6 34.3 %layer.1 = (bf16[1024,512]{1,0:T(8,128)(2,1)S(1)}, bf16[1024,512]{1,0:T(8,128)(2,1)S(1)}, bf16[1024,512]{1,0:T(8,128)(2,1)S(1)}, f32[4,8,128]{2,1,0:T(8,128)S(1)...) custom-call(bf16[1024,512]{1,0:T(8,128)(2,1)} %q_hbm.1, ...), custom_call_target="tpu_custom_call" | custom-call | tf_op jit(solution)/shard_map/layer/pallas_call | solution.py:490
  34.9 1.8 %store.1 = (bf16[1024,512]{1,0:T(8,128)(2,1)}, bf16[1024,512]{1,0:T(8,128)(2,1)}, bf16[1024,512]{1,0:T(8,128)(2,1)}, f32[4,8,128]{2,1,0:T(8,128)}) custom-call(bf16[1024,512]{1,0:T(8,128)(2,1)S(1)} %get-tuple-element.14.dq, bf16[1024,512]{1,0:T(8,128)(2,1)S(1)} %get-tuple-element.15.dk, bf16[1024,512]{1,0:T(8,128)(2,1)S(1)} %get-tuple-element.16.dv, ...), custom_call_target="tpu_custom_call" | custom-call | tf_op jit(solution)/shard_map/store/pallas_call | solution.py:566

commit v6 on v5

--- a/solution.py
+++ b/solution.py
@@ -235,7 +235,7 @@
         qh[i] = (qc.astype(F32) * hin[h, at, :]).T.astype(BF16)
         return 0
 
-    lax.fori_loop(0, heads * chunks, prepare, 0, unroll=True)
+    lax.fori_loop(0, heads * chunks, prepare, 0, unroll=4)
     kl_ref[...] = k[:, (heads - 1) * D:]
     vl_ref[...] = v[:, (heads - 1) * D:]
     scale_ref[...] = tail[heads - 1]

time: 36.8 us -> 36.9 us (level)
  no operation moved by 1% of the time
where the time goes in v6:
time: 36.9 us; the launch traced here: 36.8 us
  Pallas kernels  36.1 us (98%)
  between operations  0.64 us (2%)
    pallas_call x1, Pallas kernels, shards(): pl.pallas_call(functools.partial(layer, sizes), name='layer', out_shape=(...  34.4 us
    pallas_call x1, Pallas kernels, shards(): pl.pallas_call(store, name='store', out_shape=(whole, whole, whole, jax.S...  1.76 us

profile of v6, /device:TPU:1, one launch (start us, length us, event | category | flops | bytes accessed | tf_op | source)
XLA Modules:
  0.0 36.8 jit_solution(4101740292457846662)
XLA Ops:
  0.6 34.4 %layer.1 = (bf16[1024,512]{1,0:T(8,128)(2,1)S(1)}, bf16[1024,512]{1,0:T(8,128)(2,1)S(1)}, bf16[1024,512]{1,0:T(8,128)(2,1)S(1)}, f32[4,8,128]{2,1,0:T(8,128)S(1)...) custom-call(bf16[1024,512]{1,0:T(8,128)(2,1)} %q_hbm.1, ...), custom_call_target="tpu_custom_call" | custom-call | tf_op jit(solution)/shard_map/layer/pallas_call | solution.py:490
  35.0 1.8 %store.1 = (bf16[1024,512]{1,0:T(8,128)(2,1)}, bf16[1024,512]{1,0:T(8,128)(2,1)}, bf16[1024,512]{1,0:T(8,128)(2,1)}, f32[4,8,128]{2,1,0:T(8,128)}) custom-call(bf16[1024,512]{1,0:T(8,128)(2,1)S(1)} %get-tuple-element.14.dq, bf16[1024,512]{1,0:T(8,128)(2,1)S(1)} %get-tuple-element.15.dk, bf16[1024,512]{1,0:T(8,128)(2,1)S(1)} %get-tuple-element.16.dv, ...), custom_call_target="tpu_custom_call" | custom-call | tf_op jit(solution)/shard_map/store/pallas_call | solution.py:566
